TPU v7x, 128 devices: a whole 4x4x4 slice. The times are simulated.
128 devices in a mesh: group: 8 (over z, core), local: 16 (over y, x).
Axes of the slice: x: 4, y: 4, z: 4, core: 2. Of those that a mesh axis runs over, the one named last changes fastest.
Arguments:
- tokens: bfloat16 [512, 7168], P('local'), may hold values from -6 to 6
- cotangent: bfloat16 [512, 7168], P('local'), may hold values from -6 to 6
- gate_logits: float32 [512, 24], P('local'), may hold values from -8 to 8
- route_slot: int32 [512, 8], P('local'), may hold values from 0 to 31, all different within a row; in each aligned block of 32 rows (0 to 31, 32 to 63, ...) at most 16 rows name the same one
- slot_expert: int32 [32], replicated, may hold values from 0 to 23, as said below
- w_gate: bfloat16 [32, 7168, 1024], P('local', None, 'group')
- w_up: bfloat16 [32, 7168, 1024], P('local', None, 'group')
- w_down: bfloat16 [32, 1024, 7168], P('local', 'group'), as said below
Outputs:
- mixed: bfloat16 [512, 7168], P('local', 'group')
- grad_tokens: bfloat16 [512, 7168], P('local', 'group')
- grad_logits: float32 [512, 24], P('local')
- grad_gate: bfloat16 [32, 7168, 1024], P('local', None, 'group')
- grad_up: bfloat16 [32, 7168, 1024], P('local', None, 'group')
- grad_down: bfloat16 [32, 1024, 7168], P('local', 'group')
Inputs may be any that keep to these rules, and one draw needn't show every extreme that they name: `route_slot`: each token names 8 different slots. Of the 32 tokens of one index of local, at most 16 name one slot, a bound that some block reaches of them. `slot_expert`: the even slots hold 16 different experts, the odd slots the remaining ones, each on two odd slots: slot 2i + 1 and slot 2j + 1 hold the same expert where j = i plus or minus half the size of local (the one that stays in range). Every expert is held. `w_down`: two odd slots that hold the same expert have equal weights; entries have standard deviation 1024 ** -0.5.
All inputs are finite; a program needn't handle non-finite values.
Results may differ from a plain program's by a relative error of at most 0.019.
Values may be sent and summed in bfloat16 or wider, within the bound.
No kernel may reach another device: no remote copies, remote signals or barrier semaphores. Data moves between devices by JAX's collectives and lax.ppermute only.
A program may use at most 192 MiB of HBM per device.

v0:
```python
import jax
import jax.numpy as jnp
from jax import lax
from jax.sharding import PartitionSpec as P

ROUTE_SCALE = 2.5
CONTRACT_ONE = (((1,), (1,)), ((), ()))
CONTRACT_ZERO = (((0,), (0,)), ((), ()))


def swapped(block, axis, apart):
    count = lax.axis_size(axis)
    route = []
    for low in range(count):
        high = low | 1 << apart
        if high != low and high < count:
            route += [(low, high), (high, low)]
    return lax.ppermute(block, axis, route)


def gate_weights(logits, expert_ids, experts):
    match = expert_ids[:, :, None] == jnp.arange(experts, dtype=jnp.int32)[None, None, :]
    picked = jnp.sum(jnp.where(match, logits[:, None, :], 0.0), axis=2)
    sig = jax.nn.sigmoid(picked)
    return ROUTE_SCALE * sig / jnp.sum(sig, axis=1, keepdims=True)


def activations(rows_x, rows_g, w_g, w_u, w_d):
    first = jnp.dot(rows_x, w_g, preferred_element_type=jnp.float32)
    second = jnp.dot(rows_x, w_u, preferred_element_type=jnp.float32)
    sig = jax.nn.sigmoid(first)
    silu = first * sig
    hidden = (silu * second).astype(jnp.bfloat16)
    back = lax.dot_general(rows_g, w_d, CONTRACT_ONE, preferred_element_type=jnp.float32)
    d_first = (back * second * sig * (1.0 + first * (1.0 - sig))).astype(jnp.bfloat16)
    d_second = (back * silu).astype(jnp.bfloat16)
    return (hidden, d_first, d_second)


def weight_grads(rows_x, rows_g, hidden, d_first, d_second):
    own_gate = lax.dot_general(rows_x, d_first, CONTRACT_ZERO, preferred_element_type=jnp.float32)
    own_up = lax.dot_general(rows_x, d_second, CONTRACT_ZERO, preferred_element_type=jnp.float32)
    own_down = lax.dot_general(hidden, rows_g, CONTRACT_ZERO, preferred_element_type=jnp.float32)
    return (
        own_gate.astype(jnp.bfloat16),
        own_up.astype(jnp.bfloat16),
        own_down.astype(jnp.bfloat16),
    )


def slot_pass(rows_x, rows_g, w_g, w_u, w_d):
    hidden, d_first, d_second = activations(rows_x, rows_g, w_g, w_u, w_d)
    out_rows = jnp.dot(hidden, w_d, preferred_element_type=jnp.float32).astype(jnp.bfloat16)
    both = lax.dot_general(d_first, w_g, CONTRACT_ONE, preferred_element_type=jnp.float32)
    both = both + lax.dot_general(d_second, w_u, CONTRACT_ONE, preferred_element_type=jnp.float32)
    grad_rows = both.astype(jnp.bfloat16)
    return (out_rows, grad_rows, weight_grads(rows_x, rows_g, hidden, d_first, d_second))


def per_device(tokens, cotangent, gate_logits, route_slot, slot_expert, w_gate, w_up, w_down):
    tok = tokens.shape[0]
    width = tokens.shape[1]
    top = route_slot.shape[1]
    slots = slot_expert.shape[0]
    experts = gate_logits.shape[1]
    lines = lax.axis_size("local")
    cap = top * tok // lines
    match_slot = route_slot[:, :, None] == jnp.arange(slots, dtype=jnp.int32)[None, None, :]
    expert_ids = jnp.sum(jnp.where(match_slot, slot_expert[None, None, :], 0), axis=2)
    weights, pull_back = jax.vjp(lambda lg: gate_weights(lg, expert_ids, experts), gate_logits)
    scaled = (weights[:, :, None] * cotangent.astype(jnp.float32)[:, None, :]).astype(jnp.bfloat16)
    flat = route_slot.reshape(-1)
    onehot = (flat[:, None] == jnp.arange(slots, dtype=jnp.int32)[None, :]).astype(jnp.int32)
    rank = jnp.sum((jnp.cumsum(onehot, axis=0) - onehot) * onehot, axis=1)
    target = flat * cap + rank
    placer = (jnp.arange(slots * cap, dtype=jnp.int32)[:, None] == target[None, :]).astype(
        jnp.bfloat16
    )
    token_placer = jnp.sum(placer.reshape(slots * cap, tok, top), axis=2)
    x_buffer = jnp.dot(token_placer, tokens, preferred_element_type=jnp.float32).astype(
        jnp.bfloat16
    )
    g_buffer = jnp.dot(
        placer, scaled.reshape(tok * top, width), preferred_element_type=jnp.float32
    ).astype(jnp.bfloat16)
    x_buffer = x_buffer.reshape(lines, 2 * cap, width)
    g_buffer = g_buffer.reshape(lines, 2 * cap, width)
    got_x, got_g = (
        lax.all_to_all(x_buffer, "local", split_axis=0, concat_axis=0, tiled=True),
        lax.all_to_all(g_buffer, "local", split_axis=0, concat_axis=0, tiled=True),
    )
    got_x = got_x.reshape(lines, 2, cap, width)
    got_g = got_g.reshape(lines, 2, cap, width)
    rows_cold_x = got_x[:, 0].reshape(lines * cap, width)
    rows_cold_g = got_g[:, 0].reshape(lines * cap, width)
    rows_hot_x = got_x[:, 1].reshape(lines * cap, width)
    rows_hot_g = got_g[:, 1].reshape(lines * cap, width)
    out_cold, dx_cold, grads_cold = slot_pass(
        rows_cold_x, rows_cold_g, w_gate[0], w_up[0], w_down[0]
    )
    out_hot, dx_hot, grads_hot = slot_pass(rows_hot_x, rows_hot_g, w_gate[1], w_up[1], w_down[1])
    outs_back = jnp.stack(
        [out_cold.reshape(lines, cap, width), out_hot.reshape(lines, cap, width)], axis=1
    )
    dxs_back = jnp.stack(
        [dx_cold.reshape(lines, cap, width), dx_hot.reshape(lines, cap, width)], axis=1
    )
    outs_back = outs_back.reshape(lines, 2 * cap, width)
    dxs_back = dxs_back.reshape(lines, 2 * cap, width)
    home_out, home_dx = (
        lax.all_to_all(outs_back, "local", split_axis=0, concat_axis=0, tiled=True),
        lax.all_to_all(dxs_back, "local", split_axis=0, concat_axis=0, tiled=True),
    )
    home_out = home_out.reshape(slots * cap, width)
    home_dx = home_dx.reshape(slots * cap, width)
    gathered = lax.dot_general(placer, home_out, CONTRACT_ZERO, preferred_element_type=jnp.float32)
    gathered = gathered.reshape(tok, top, width)
    partial_out = jnp.sum(weights[:, :, None] * gathered, axis=1)
    partial_dx = lax.dot_general(
        token_placer, home_dx, CONTRACT_ZERO, preferred_element_type=jnp.float32
    )
    partial_dots = jnp.sum(cotangent.astype(jnp.float32)[:, None, :] * gathered, axis=2)
    mixed, grad_tokens = (
        lax.psum_scatter(
            partial_out.astype(jnp.bfloat16), "group", scatter_dimension=1, tiled=True
        ).astype(jnp.float32),
        lax.psum_scatter(
            partial_dx.astype(jnp.bfloat16), "group", scatter_dimension=1, tiled=True
        ).astype(jnp.float32),
    )
    gate_dots = lax.psum(partial_dots, "group")
    grad_logits = pull_back(gate_dots)[0]
    partner_bit = lax.axis_size("local").bit_length() - 2
    other = swapped((grads_hot[0], grads_hot[1], grads_hot[2]), "local", partner_bit)
    joined = [
        (mine.astype(jnp.float32) + theirs.astype(jnp.float32)).astype(jnp.bfloat16)
        for mine, theirs in zip(grads_hot, other)
    ]
    grad_gate = jnp.stack([grads_cold[0], joined[0]], axis=0)
    grad_up = jnp.stack([grads_cold[1], joined[1]], axis=0)
    grad_down = jnp.stack([grads_cold[2], joined[2]], axis=0)
    return (
        mixed.astype(jnp.bfloat16),
        grad_tokens.astype(jnp.bfloat16),
        grad_logits,
        grad_gate,
        grad_up,
        grad_down,
    )


def solution(mesh):
    return jax.shard_map(
        per_device,
        mesh=mesh,
        in_specs=(
            P("local", None),
            P("local", None),
            P("local", None),
            P("local", None),
            P(),
            P("local", None, "group"),
            P("local", None, "group"),
            P("local", "group", None),
        ),
        out_specs=(
            P("local", "group"),
            P("local", "group"),
            P("local", None),
            P("local", None, "group"),
            P("local", None, "group"),
            P("local", "group", None),
        ),
        check_vma=False,
    )
```

profile of v0, /device:TPU:0, one launch (start us, length us, event | category | flops | bytes accessed | tf_op | source)
XLA Modules:
  0.0 620.1 jit_solution(16297483419287537097)
XLA Ops:
  9.5 5.0 convolution_convert_fusion.1
  14.5 7.3 %all-to-all-start = ((bf16[16,32,7168]{2,1,0:T(8,128)(2,1)}), bf16[16,32,7168]{2,1,0:T(8,128)(2,1)}, u32[]{:S(2)}, u32[]{:S(2)}) async-start(bf16[16,32,7168]{2,1,0:T(8,128)(2,1)} %bitcast.142), calls=%async_computation | async-start | bytes 14680064 | tf_op jit(solution)/shard_map/all_to_all | solution.py:89
  22.9 5.2 convolution_convert_fusion
  28.1 102.3 %all-to-all-done = bf16[16,32,7168]{2,1,0:T(8,128)(2,1)} async-done(((bf16[16,32,7168]{2,1,0:T(8,128)(2,1)}), bf16[16,32,7168]{2,1,0:T(8,128)(2,1)}, u32[]{:S(2)}, u32[]{:S(2)}) %all-to-all-start) | async-done | bytes 7340064 | tf_op jit(solution)/shard_map/all_to_all | solution.py:89
  130.5 5.8 all-to-all-start.2
  136.3 3.8 fusion.60
  140.5 1.1 fusion.16
  141.6 3.3 copy-done.14
  144.9 1.1 fusion.20
  146.0 1.1 fusion.26
  147.2 1.1 fusion.30
  148.3 94.5 %all-to-all-done.2 = bf16[16,32,7168]{2,1,0:T(8,128)(2,1)} async-done(((bf16[16,32,7168]{2,1,0:T(8,128)(2,1)}), bf16[16,32,7168]{2,1,0:T(8,128)(2,1)}, u32[]{:S(2)}, u32[]{:S(2)}) %all-to-all-start.2) | async-done | bytes 7340064 | tf_op jit(solution)/shard_map/all_to_all | solution.py:90
  242.8 3.8 fusion.59
  248.1 3.3 copy-done.15
  255.7 1.1 fusion
  256.8 1.1 fusion.1
  258.0 3.8 pad_maximum_fusion.1
  261.8 4.9 all-to-all-start.3
  266.7 4.2 convolution_convert_fusion.4
  270.9 3.4 collective-permute-start.2
  274.2 2.5 fusion.3
  276.7 2.4 fusion.2
  279.1 2.4 convolution_convert_fusion.6
  281.5 1.2 convolution_convert_fusion.8
  283.6 1.9 fusion.4
  285.6 3.4 collective-permute-start
  291.2 3.7 pad_maximum_fusion
  294.9 77.8 %all-to-all-done.3 = bf16[16,32,7168]{2,1,0:T(8,128)(2,1)} async-done(((bf16[16,32,7168]{2,1,0:T(8,128)(2,1)}), bf16[16,32,7168]{2,1,0:T(8,128)(2,1)}, u32[]{:S(2)}, u32[]{:S(2)}) %all-to-all-start.3) | async-done | bytes 7340064 | tf_op jit(solution)/shard_map/all_to_all | solution.py:112
  372.7 10.7 %all-to-all-start.1 = ((bf16[16,32,7168]{2,1,0:T(8,128)(2,1)}), bf16[16,32,7168]{2,1,0:T(8,128)(2,1)}, u32[]{:S(2)}, u32[]{:S(2)}) async-start(bf16[16,32,7168]{2,1,0:T(8,128)(2,1)} %bitcast.144), calls=%async_computation.1 | async-start | bytes 14680064 | tf_op jit(solution)/shard_map/all_to_all | solution.py:111
  383.8 58.0 %collective-permute-done.2 = bf16[128,7168]{1,0:T(8,128)(2,1)} collective-permute-done((bf16[128,7168]{1,0:T(8,128)(2,1)}, bf16[128,7168]{1,0:T(8,128)(2,1)}, u32[]{:S(2)}, u32[]{:S(2)}) %collective-permute-start.2) | collective-permute-done | bytes 1835040 | tf_op jit(solution)/shard_map/ppermute | solution.py:18
  441.8 2.5 fusion.11
  444.3 2.2 pad_maximum_fusion.4
  446.5 44.4 %collective-permute-done.1 = bf16[7168,128]{1,0:T(8,128)(2,1)} collective-permute-done((bf16[7168,128]{1,0:T(8,128)(2,1)}, bf16[7168,128]{1,0:T(8,128)(2,1)}, u32[]{:S(2)}, u32[]{:S(2)}) %collective-permute-start.1) | collective-permute-done | bytes 1835040 | tf_op jit(solution)/shard_map/ppermute | solution.py:18
  490.9 3.7 fusion.10
  494.6 35.5 %collective-permute-done = bf16[7168,128]{1,0:T(8,128)(2,1)} collective-permute-done((bf16[7168,128]{1,0:T(8,128)(2,1)S(1)}, bf16[7168,128]{1,0:T(8,128)(2,1)}, u32[]{:S(2)}, u32[]{:S(2)}) %collective-permute-start) | collective-permute-done | bytes 1835040 | tf_op jit(solution)/shard_map/ppermute | solution.py:18
  530.2 3.3 fusion.9
  533.4 4.5 convolution_convert_fusion.10
  537.9 1.7 copy.64
  539.8 3.7 pad_maximum_fusion.3
  543.5 4.1 all-to-all-done.1
  547.5 7.9 %multiply_reduce_fusion = (f32[32,8]{1,0:T(8,128)S(1)}, bf16[32,7168]{1,0:T(8,128)(2,1)S(1)}) fusion(f32[32,7168]{1,0:T(8,128)S(1)} %convert_element_type.121, f32[32,8]{1,0:T(8,128)S(1)} %copy.51, bf16[512,7168,1]{1,0,2:T(8,128)(2,1)} %bitcast.18, s32[256]{0:T(256)S(1)} %multiply_add_fusion.1), kind=kOutput, calls=%fused_computation.22 | convolution fusion | flops 1886289664 | bytes 8719360 | tf_op jit(solution)/shard_map/dot_general | solution.py:116
  555.5 1.6 copy.62
  557.4 3.7 pad_maximum_fusion.2
  561.2 14.0 %psum.7 = f32[32,8]{0,1:T(8,128)S(1)} all-reduce(f32[32,8]{0,1:T(8,128)S(1)} %copy.61), channel_id=1, replica_groups=mesh['group'=8,'local'=16] {'group'}, use_global_device_ids=true, to_apply=%region_11.12 | all-reduce | flops 256 | bytes 2048 | tf_op jit(solution)/shard_map/psum | solution.py:131
  575.8 1.3 reduce-scatter.9.cloned.1.call-done
  577.2 1.7 copy.65
  578.8 32.8 %reduce-scatter.7.cloned.1.call-done = bf16[896,32]{1,0:T(8,128)(2,1)} async-done(((bf16[7168,32]{1,0:T(8,128)(2,1)}), bf16[896,32]{1,0:T(8,128)(2,1)}) %reduce-scatter.7.cloned.1.call-update) | async-done | bytes 57360
  611.6 1.7 copy.63
  (78 shorter events, 14.2 us)
Async XLA Ops:
  7.2 2.3 copy-start
  14.5 7.3 %copy-start.20 = (s32[32]{0:T(128)S(1)}, s32[32]{0:T(128)}, u32[]{:S(2)}) copy-start(s32[32]{0:T(128)} %param.12) | copy-start | bytes 388
  14.5 8.1 %copy-start.19 = (f32[32,24]{0,1:T(8,128)S(1)}, f32[32,24]{0,1:T(8,128)}, u32[]{:S(2)}) copy-start(f32[32,24]{0,1:T(8,128)} %param.10) | copy-start | bytes 9220
  14.5 8.3 %copy-start.18 = (bf16[32,7168]{1,0:T(8,128)(2,1)S(1)}, bf16[32,7168]{1,0:T(8,128)(2,1)}, u32[]{:S(2)}) copy-start(bf16[32,7168]{1,0:T(8,128)(2,1)} %param.9) | copy-start | bytes 1376260
  14.5 116.0 %all-to-all-start = ((bf16[16,32,7168]{2,1,0:T(8,128)(2,1)}), bf16[16,32,7168]{2,1,0:T(8,128)(2,1)}, u32[]{:S(2)}, u32[]{:S(2)}) async-start(bf16[16,32,7168]{2,1,0:T(8,128)(2,1)} %bitcast.142), calls=%async_computation | async-start | bytes 14680064 | tf_op jit(solution)/shard_map/all_to_all | solution.py:89
  130.5 112.4 %all-to-all-start.2 = ((bf16[16,32,7168]{2,1,0:T(8,128)(2,1)}), bf16[16,32,7168]{2,1,0:T(8,128)(2,1)}, u32[]{:S(2)}, u32[]{:S(2)}) async-start(bf16[16,32,7168]{2,1,0:T(8,128)(2,1)} %bitcast.143), calls=%async_computation.2 | async-start | bytes 14680064 | tf_op jit(solution)/shard_map/all_to_all | solution.py:90
  136.3 4.2 copy-start.12
  140.1 5.9 copy-start.4
  140.1 7.0 %copy-start.2 = (bf16[16,1,16,7168]{3,2,1,0:T(8,128)(2,1)}, bf16[16,1,16,7168]{3,2,1,0:T(8,128)(2,1)S(1)}, u32[]{:S(2)}) copy-start(bf16[16,1,16,7168]{3,2,1,0:T(8,128)(2,1)S(1)} %get-tuple-element.10) | copy-start | bytes 11010052
  140.1 4.8 copy-start.14
  242.8 4.2 copy-start.16
  246.6 5.9 copy-start.6
  246.6 5.9 copy-start.8
  246.6 4.8 copy-start.15
  253.7 2.0 copy-start.13
  261.8 111.0 %all-to-all-start.3 = ((bf16[16,32,7168]{2,1,0:T(8,128)(2,1)}), bf16[16,32,7168]{2,1,0:T(8,128)(2,1)}, u32[]{:S(2)}, u32[]{:S(2)}) async-start(bf16[16,32,7168]{2,1,0:T(8,128)(2,1)} %bitcast.145), calls=%async_computation.3 | async-start | bytes 14680064 | tf_op jit(solution)/shard_map/all_to_all | solution.py:112
  266.6 7.6 %copy-start.3 = (bf16[16,1,16,7168]{3,2,1,0:T(8,128)(2,1)S(1)}, bf16[16,1,16,7168]{3,2,1,0:T(8,128)(2,1)}, u32[]{:S(2)}) copy-start(bf16[16,1,16,7168]{3,2,1,0:T(8,128)(2,1)} %copy-done.2) | copy-start | bytes 11010052
  270.9 170.9 %collective-permute-start.2 = (bf16[128,7168]{1,0:T(8,128)(2,1)}, bf16[128,7168]{1,0:T(8,128)(2,1)}, u32[]{:S(2)}, u32[]{:S(2)}) collective-permute-start(bf16[128,7168]{1,0:T(8,128)(2,1)} %convolution_convert_fusion.4), channel_id=1, source_target_pairs={{0,8},{8,0},{1,9},{9,1},{2,10},{10,2},{3,11},{11,3},{4,12},{12,4},... | collective-permute-start | bytes 5505032 | tf_op jit(solution)/shard_map/ppermute | solution.py:18
  276.7 2.4 copy-start.5
  281.5 2.0 copy-start.7
  282.7 6.3 %copy-start.17 = (bf16[2,128,7168]{2,1,0:T(8,128)(2,1)S(1)}, bf16[2,128,7168]{2,1,0:T(8,128)(2,1)}, u32[]{:S(2)}) copy-start(bf16[2,128,7168]{2,1,0:T(8,128)(2,1)} %param.15) | copy-start | bytes 11010052
  285.5 205.4 %collective-permute-start.1 = (bf16[7168,128]{1,0:T(8,128)(2,1)}, bf16[7168,128]{1,0:T(8,128)(2,1)}, u32[]{:S(2)}, u32[]{:S(2)}) collective-permute-start(bf16[7168,128]{1,0:T(8,128)(2,1)} %convolution_convert_fusion.6), channel_id=1, source_target_pairs={{0,8},{8,0},{1,9},{9,1},{2,10},{10,2},{3,11},{11,3},{4,12},{12,4},... | collective-permute-start | bytes 5505032 | tf_op jit(solution)/shard_map/ppermute | solution.py:18
  285.6 244.5 %collective-permute-start = (bf16[7168,128]{1,0:T(8,128)(2,1)S(1)}, bf16[7168,128]{1,0:T(8,128)(2,1)}, u32[]{:S(2)}, u32[]{:S(2)}) collective-permute-start(bf16[7168,128]{1,0:T(8,128)(2,1)S(1)} %convolution_convert_fusion.8), channel_id=1, source_target_pairs={{0,8},{8,0},{1,9},{9,1},{2,10},{10,2},{3,11},{11,3},{4,12},{12,4},... | collective-permute-start | bytes 5505032 | tf_op jit(solution)/shard_map/ppermute | solution.py:18
  372.7 174.8 %all-to-all-start.1 = ((bf16[16,32,7168]{2,1,0:T(8,128)(2,1)}), bf16[16,32,7168]{2,1,0:T(8,128)(2,1)}, u32[]{:S(2)}, u32[]{:S(2)}) async-start(bf16[16,32,7168]{2,1,0:T(8,128)(2,1)} %bitcast.144), calls=%async_computation.1 | async-start | bytes 14680064 | tf_op jit(solution)/shard_map/all_to_all | solution.py:111
  383.5 193.7 %reduce-scatter.9.cloned.1.call-start = ((), (), s32[]{:S(2)}) async-start(), calls=%async_computation.7 | async-start | bytes 2064384
  383.8 60.5 %copy-start.11 = (bf16[1,128,7168]{2,1,0:T(8,128)(2,1)S(1)}, bf16[1,128,7168]{2,1,0:T(8,128)(2,1)}, u32[]{:S(2)}) copy-start(bf16[1,128,7168]{2,1,0:T(8,128)(2,1)} %fusion.4) | copy-start | bytes 5505028
  537.9 1.9 copy-start.10
  539.6 72.0 %reduce-scatter.7.cloned.1.call-start = ((), (), s32[]{:S(2)}) async-start(), calls=%async_computation.6 | async-start | bytes 2064384
  555.5 1.9 copy-start.9
  557.4 55.9 %copy-start.1 = (bf16[32,7168]{1,0:T(8,128)(2,1)S(1)}, bf16[32,7168]{1,0:T(8,128)(2,1)}, u32[]{:S(2)}) copy-start(bf16[32,7168]{1,0:T(8,128)(2,1)} %param.8) | copy-start | bytes 1376260
Sparse Core Ops, SparseCore 0:
  539.7 37.4 reduce-scatter.8
  579.6 31.9 reduce-scatter.6
where the time goes:
time: 621 us; the launch traced here: 620 us
  waiting for transfers between devices  451 us (73%)
  matrix products  50.6 us (8%)
  starting transfers between devices  36 us (6%)
  other arithmetic  29 us (5%)
  local copies, waits for them, and re-layouts  25.2 us (4%)
  between operations  14.5 us (2%)
  blocking collectives  14 us (2%)
    ppermute x3, waiting for transfers between devices, swapped(): return lax.ppermute(block, axis, route)  138 us
    all_to_all x1, waiting for transfers between devices, per_device(): lax.all_to_all(x_buffer, 'local', split_axis=0, concat_axis=0, tiled=True)  102 us
    all_to_all x1, waiting for transfers between devices, per_device(): lax.all_to_all(g_buffer, 'local', split_axis=0, concat_axis=0, tiled=True)  94.5 us
    all_to_all x1, waiting for transfers between devices, per_device(): lax.all_to_all(dxs_back, 'local', split_axis=0, concat_axis=0, tiled=True)  77.8 us
    unnamed x4, waiting for transfers between devices  34.1 us
    unnamed x47, local copies, waits for them, and re-layouts  17 us
    psum x1, blocking collectives, per_device(): gate_dots = lax.psum(partial_dots, 'group')  14 us
  transfers between devices with their start and end apart: 9, of which 9 were waited for; matrix products, arithmetic and copies ran while one was open for 12% of the time, Pallas kernels for 0%

commit v1 on v0

--- a/solution.py
+++ b/solution.py
@@ -6,6 +6,35 @@
 ROUTE_SCALE = 2.5
 CONTRACT_ONE = (((1,), (1,)), ((), ()))
 CONTRACT_ZERO = (((0,), (0,)), ((), ()))
+
+
+def feed_positions_for(sample, in_dim, array_in):
+    step_out, oldest = (sample.shape[:in_dim], sample.shape[in_dim + 1 :])
+    piece_out = sample.reshape(*step_out, array_in, -1, *oldest)
+    now = jnp.moveaxis(piece_out, in_dim, 0)
+    return now
+
+
+def mix_sheets_now(incoming_x, dim_i):
+    u_next = list(incoming_x.shape[1:])
+    u_next[dim_i] *= incoming_x.shape[0]
+    prior = jnp.moveaxis(incoming_x, 0, dim_i).reshape(u_next)
+    return prior
+
+
+def pack_the_group(inner_x, device_axis, my_data, array_here):
+    small = lax.axis_size(device_axis)
+    f_now = lax.axis_index(device_axis)
+    left_arr, even = (small, f_now)
+    base_arr = feed_positions_for(inner_x, my_data, left_arr)
+    rows = [base_arr[even]]
+    for s in [*range(1, left_arr)]:
+        e_next = base_arr[even ^ s]
+        rows.append(lax.ppermute(e_next, device_axis, [(q, q ^ s) for q in range(left_arr)]))
+    answer = jnp.stack(rows, axis=0)
+    base_arr = answer[even ^ jnp.arange(left_arr)]
+    carry_in = mix_sheets_now(base_arr, array_here)
+    return carry_in
 
 
 def swapped(block, axis, apart):
@@ -86,7 +115,7 @@
     x_buffer = x_buffer.reshape(lines, 2 * cap, width)
     g_buffer = g_buffer.reshape(lines, 2 * cap, width)
     got_x, got_g = (
-        lax.all_to_all(x_buffer, "local", split_axis=0, concat_axis=0, tiled=True),
+        pack_the_group(x_buffer, "local", 0, 0),
         lax.all_to_all(g_buffer, "local", split_axis=0, concat_axis=0, tiled=True),
     )
     got_x = got_x.reshape(lines, 2, cap, width)

time: 621 us -> 660 us (1.063); the launches traced: 620 us -> 651 us
  starting transfers between devices: 36 us -> 179 us
  waiting for transfers between devices: 451 us -> 315 us
  local copies, waits for them, and re-layouts: 25.2 us -> 49.4 us
    ppermute x3, waiting for transfers between devices: 138 us -> 0.01 us  [swapped(): return lax.ppermute(block, axis, route)]
    ppermute x0 -> x15, waiting for transfers between devices: none -> 134 us  [pack_the_group(): lax.ppermute(e_next, device_axis, [(q, q ^ s) for q in range(left_arr)])]
    all_to_all x1 -> x0, waiting for transfers between devices: 102 us -> none  [per_device(): lax.all_to_all(x_buffer, 'local', split_axis=0, concat_axis=0, tiled=True)]
    all_to_all x1, waiting for transfers between devices: 94.5 us -> 0.01 us  [per_device(): lax.all_to_all(g_buffer, 'local', split_axis=0, concat_axis=0, tiled=True)]
    all_to_all x1, starting transfers between devices: 10.7 us -> 95.1 us  [per_device(): lax.all_to_all(outs_back, 'local', split_axis=0, concat_axis=0, tiled=True)]
    all_to_all x1, waiting for transfers between devices: 4.05 us -> 87 us  [per_device(): lax.all_to_all(outs_back, 'local', split_axis=0, concat_axis=0, tiled=True)]
    ppermute x0 -> x15, starting transfers between devices: none -> 57.3 us  [pack_the_group(): lax.ppermute(e_next, device_axis, [(q, q ^ s) for q in range(left_arr)])]
    unnamed x4, waiting for transfers between devices: 34.1 us -> 12.9 us
  transfers between devices with their start and end apart: 9 -> 23, of which waited for: 9 -> 6; matrix products, arithmetic and copies ran while one was open for 12% -> 14% of each run, Pallas kernels for 0% -> 0%
where the time goes in v1:
time: 660 us; the launch traced here: 651 us
  waiting for transfers between devices  315 us (48%)
  starting transfers between devices  179 us (27%)
  local copies, waits for them, and re-layouts  49.4 us (7%)
  matrix products  47.9 us (7%)
  other arithmetic  30 us (5%)
  blocking collectives  14.9 us (2%)
  between operations  14.9 us (2%)
    ppermute x15, waiting for transfers between devices, pack_the_group(): lax.ppermute(e_next, device_axis, [(q, q ^ s) for q in range(left_arr)])  134 us
    all_to_all x1, starting transfers between devices, per_device(): lax.all_to_all(outs_back, 'local', split_axis=0, concat_axis=0, tiled=True)  95.1 us
    all_to_all x1, waiting for transfers between devices, per_device(): lax.all_to_all(outs_back, 'local', split_axis=0, concat_axis=0, tiled=True)  87 us
    all_to_all x1, waiting for transfers between devices, per_device(): lax.all_to_all(dxs_back, 'local', split_axis=0, concat_axis=0, tiled=True)  80.9 us
    ppermute x15, starting transfers between devices, pack_the_group(): lax.ppermute(e_next, device_axis, [(q, q ^ s) for q in range(left_arr)])  57.3 us
    unnamed x73, local copies, waits for them, and re-layouts  30.2 us
    psum x1, blocking collectives, per_device(): gate_dots = lax.psum(partial_dots, 'group')  14.9 us
  transfers between devices with their start and end apart: 23, of which 6 were waited for; matrix products, arithmetic and copies ran while one was open for 14% of the time, Pallas kernels for 0%

profile of v1, /device:TPU:0, one launch (start us, length us, event | category | flops | bytes accessed | tf_op | source)
XLA Modules:
  0.0 651.3 jit_solution(8438356610027915209)
XLA Ops:
  9.6 2.1 convolution_convert_fusion.1
  11.7 3.1 dynamic-slice_bitcast_fusion
  16.4 2.7 collective-permute-start.1
  19.5 1.7 collective-permute-start.3
  23.4 5.2 convolution_convert_fusion
  28.7 8.0 %all-to-all-start.1 = ((bf16[16,32,7168]{2,1,0:T(8,128)(2,1)}), bf16[16,32,7168]{2,1,0:T(8,128)(2,1)}, u32[]{:S(2)}, u32[]{:S(2)}) async-start(bf16[16,32,7168]{2,1,0:T(8,128)(2,1)} %bitcast.206), calls=%async_computation.1 | async-start | bytes 14680064 | tf_op jit(solution)/shard_map/all_to_all | solution.py:119
  37.5 4.3 collective-permute-start.5
  41.8 1.9 bitcast_dynamic-update-slice_fusion.14
  45.7 3.0 collective-permute-start.7
  50.3 5.4 collective-permute-done.4
  57.0 107.4 %collective-permute-done.5 = bf16[1,32,7168]{2,1,0:T(8,128)(2,1)S(1)} collective-permute-done((bf16[1,32,7168]{2,1,0:T(8,128)(2,1)}, bf16[1,32,7168]{2,1,0:T(8,128)(2,1)S(1)}, u32[]{:S(2)}, u32[]{:S(2)}) %collective-permute-start.5) | collective-permute-done | bytes 458784 | tf_op jit(solution)/shard_map/ppermute | solution.py:33
  164.4 14.5 %collective-permute-start.10 = (bf16[1,32,7168]{2,1,0:T(8,128)(2,1)S(1)}, bf16[1,32,7168]{2,1,0:T(8,128)(2,1)S(1)}, u32[]{:S(2)}, u32[]{:S(2)}) collective-permute-start(bf16[1,32,7168]{2,1,0:T(8,128)(2,1)S(1)} %copy-done.23), channel_id=1, source_target_pairs={{0,11},{1,10},{2,9},{3,8},{4,15},{5,14},{6,13},{7,12},{8,3},{9,2},... | collective-permute-start | bytes 1376264 | tf_op jit(solution)/shard_map/ppermute | solution.py:33
  180.6 8.4 %collective-permute-start.12 = (bf16[1,32,7168]{2,1,0:T(8,128)(2,1)S(1)}, bf16[1,32,7168]{2,1,0:T(8,128)(2,1)S(1)}, u32[]{:S(2)}, u32[]{:S(2)}) collective-permute-start(bf16[1,32,7168]{2,1,0:T(8,128)(2,1)S(1)} %copy-done.21), channel_id=1, source_target_pairs={{0,13},{1,12},{2,15},{3,14},{4,9},{5,8},{6,11},{7,10},{8,5},{9,4},... | collective-permute-start | bytes 1376264 | tf_op jit(solution)/shard_map/ppermute | solution.py:33
  189.9 8.9 %collective-permute-start.13 = (bf16[1,32,7168]{2,1,0:T(8,128)(2,1)S(1)}, bf16[1,32,7168]{2,1,0:T(8,128)(2,1)S(1)}, u32[]{:S(2)}, u32[]{:S(2)}) collective-permute-start(bf16[1,32,7168]{2,1,0:T(8,128)(2,1)S(1)} %copy-done.20), channel_id=1, source_target_pairs={{0,14},{1,15},{2,12},{3,13},{4,10},{5,11},{6,8},{7,9},{8,6},{9,7},... | collective-permute-start | bytes 1376264 | tf_op jit(solution)/shard_map/ppermute | solution.py:33
  199.6 9.9 %collective-permute-start.14 = (bf16[1,32,7168]{2,1,0:T(8,128)(2,1)S(1)}, bf16[1,32,7168]{2,1,0:T(8,128)(2,1)S(1)}, u32[]{:S(2)}, u32[]{:S(2)}) collective-permute-start(bf16[1,32,7168]{2,1,0:T(8,128)(2,1)S(1)} %copy-done.19), channel_id=1, source_target_pairs={{0,15},{1,14},{2,13},{3,12},{4,11},{5,10},{6,9},{7,8},{8,7},{9,6},... | collective-permute-start | bytes 1376264 | tf_op jit(solution)/shard_map/ppermute | solution.py:33
  211.2 21.2 %collective-permute-done.11 = bf16[1,32,7168]{2,1,0:T(8,128)(2,1)S(1)} collective-permute-done((bf16[1,32,7168]{2,1,0:T(8,128)(2,1)S(1)}, bf16[1,32,7168]{2,1,0:T(8,128)(2,1)S(1)}, u32[]{:S(2)}, u32[]{:S(2)}) %collective-permute-start.11) | collective-permute-done | bytes 458784 | tf_op jit(solution)/shard_map/ppermute | solution.py:33
  235.6 7.0 %gather_fusion = bf16[16,32,7168]{2,1,0:T(8,128)(2,1)} fusion(bf16[16,32,7168]{2,1,0:T(8,128)(2,1)} %bitcast.218, s32[1024]{0:T(1024)S(1)} %pad_clamp_fusion), kind=kCustom, calls=%fused_computation | custom fusion | bytes 14680128 | tf_op jit(solution)/shard_map/gather | solution.py:35
  242.6 3.8 fusion.61
  247.9 3.2 copy-done.14
  254.6 3.8 fusion.60
  259.9 3.3 copy-done.15
  270.0 3.6 pad_maximum_fusion.1
  273.5 11.9 %all-to-all-start.2 = ((bf16[16,32,7168]{2,1,0:T(8,128)(2,1)}), bf16[16,32,7168]{2,1,0:T(8,128)(2,1)}, u32[]{:S(2)}, u32[]{:S(2)}) async-start(bf16[16,32,7168]{2,1,0:T(8,128)(2,1)} %bitcast.208), calls=%async_computation.2 | async-start | bytes 14680064 | tf_op jit(solution)/shard_map/all_to_all | solution.py:141
  285.5 4.2 convolution_convert_fusion.4
  289.6 3.4 collective-permute-start.17
  293.0 2.5 fusion.3
  295.5 2.4 fusion.2
  297.9 2.4 convolution_convert_fusion.6
  302.3 1.9 fusion.4
  304.4 3.4 collective-permute-start.15
  310.0 3.7 pad_maximum_fusion
  313.7 80.9 %all-to-all-done.2 = bf16[16,32,7168]{2,1,0:T(8,128)(2,1)} async-done(((bf16[16,32,7168]{2,1,0:T(8,128)(2,1)}), bf16[16,32,7168]{2,1,0:T(8,128)(2,1)}, u32[]{:S(2)}, u32[]{:S(2)}) %all-to-all-start.2) | async-done | bytes 7340064 | tf_op jit(solution)/shard_map/all_to_all | solution.py:141
  394.5 95.1 %all-to-all-start = ((bf16[16,32,7168]{2,1,0:T(8,128)(2,1)}), bf16[16,32,7168]{2,1,0:T(8,128)(2,1)}, u32[]{:S(2)}, u32[]{:S(2)}) async-start(bf16[16,32,7168]{2,1,0:T(8,128)(2,1)} %bitcast.207), calls=%async_computation | async-start | bytes 14680064 | tf_op jit(solution)/shard_map/all_to_all | solution.py:140
  489.9 2.6 fusion.11
  492.5 2.2 pad_maximum_fusion.4
  494.7 3.8 fusion.10
  498.5 3.3 fusion.9
  501.7 4.4 convolution_convert_fusion.10
  506.2 1.7 copy.64
  508.1 3.7 pad_maximum_fusion.3
  511.8 87.0 %all-to-all-done = bf16[16,32,7168]{2,1,0:T(8,128)(2,1)} async-done(((bf16[16,32,7168]{2,1,0:T(8,128)(2,1)}), bf16[16,32,7168]{2,1,0:T(8,128)(2,1)}, u32[]{:S(2)}, u32[]{:S(2)}) %all-to-all-start) | async-done | bytes 7340064 | tf_op jit(solution)/shard_map/all_to_all | solution.py:140
  598.8 7.9 %multiply_reduce_fusion = (f32[32,8]{1,0:T(8,128)S(1)}, bf16[32,7168]{1,0:T(8,128)(2,1)S(1)}) fusion(f32[32,7168]{1,0:T(8,128)S(1)} %convert_element_type.121, f32[32,8]{1,0:T(8,128)S(1)} %copy.51, bf16[512,7168,1]{1,0,2:T(8,128)(2,1)} %bitcast.50, s32[256]{0:T(256)S(1)} %multiply_add_fusion.1), kind=kOutput, calls=%fused_computation.23 | convolution fusion | flops 1886289664 | bytes 8719360 | tf_op jit(solution)/shard_map/dot_general | solution.py:145
  606.7 1.6 copy.62
  608.6 3.7 pad_maximum_fusion.2
  612.4 14.9 %psum.7 = f32[32,8]{0,1:T(8,128)S(1)} all-reduce(f32[32,8]{0,1:T(8,128)S(1)} %copy.61), channel_id=1, replica_groups=mesh['group'=8,'local'=16] {'group'}, use_global_device_ids=true, to_apply=%region_11.12 | all-reduce | flops 256 | bytes 2048 | tf_op jit(solution)/shard_map/psum | solution.py:160
  628.0 1.7 copy.65
  629.6 12.9 %reduce-scatter.7.cloned.1.call-done = bf16[896,32]{1,0:T(8,128)(2,1)} async-done(((bf16[7168,32]{1,0:T(8,128)(2,1)}), bf16[896,32]{1,0:T(8,128)(2,1)}) %reduce-scatter.7.cloned.1.call-update) | async-done | bytes 57360
  642.5 1.7 copy.63
  (137 shorter events, 39.4 us)
Async XLA Ops:
  7.2 2.4 copy-start
  11.7 9.6 %copy-start.26 = (s32[32]{0:T(128)S(1)}, s32[32]{0:T(128)}, u32[]{:S(2)}) copy-start(s32[32]{0:T(128)} %param.12) | copy-start | bytes 388
  11.7 10.4 %copy-start.25 = (f32[32,24]{0,1:T(8,128)S(1)}, f32[32,24]{0,1:T(8,128)}, u32[]{:S(2)}) copy-start(f32[32,24]{0,1:T(8,128)} %param.10) | copy-start | bytes 9220
  14.8 21.9 %collective-permute-start = (bf16[1,32,7168]{2,1,0:T(8,128)(2,1)}, bf16[1,32,7168]{2,1,0:T(8,128)(2,1)S(1)}, u32[]{:S(2)}, u32[]{:S(2)}) collective-permute-start(bf16[1,32,7168]{2,1,0:T(8,128)(2,1)} %get-tuple-element.26), channel_id=1, source_target_pairs={{0,1},{1,0},{2,3},{3,2},{4,5},{5,4},{6,7},{7,6},{8,9},{9,8},{10,11... | collective-permute-start | bytes 1376264 | tf_op jit(solution)/shard_map/ppermute | solution.py:33
  16.4 27.3 %collective-permute-start.1 = (bf16[1,32,7168]{2,1,0:T(8,128)(2,1)}, bf16[1,32,7168]{2,1,0:T(8,128)(2,1)S(1)}, u32[]{:S(2)}, u32[]{:S(2)}) collective-permute-start(bf16[1,32,7168]{2,1,0:T(8,128)(2,1)} %get-tuple-element.25), channel_id=1, source_target_pairs={{0,2},{1,3},{2,0},{3,1},{4,6},{5,7},{6,4},{7,5},{8,10},{9,11},{10,... | collective-permute-start | bytes 1376264 | tf_op jit(solution)/shard_map/ppermute | solution.py:33
  19.1 26.6 %collective-permute-start.2 = (bf16[1,32,7168]{2,1,0:T(8,128)(2,1)}, bf16[1,32,7168]{2,1,0:T(8,128)(2,1)S(1)}, u32[]{:S(2)}, u32[]{:S(2)}) collective-permute-start(bf16[1,32,7168]{2,1,0:T(8,128)(2,1)} %get-tuple-element.24), channel_id=1, source_target_pairs={{0,3},{1,2},{2,1},{3,0},{4,7},{5,6},{6,5},{7,4},{8,11},{9,10},{10,... | collective-permute-start | bytes 1376264 | tf_op jit(solution)/shard_map/ppermute | solution.py:33
  19.5 30.0 %collective-permute-start.3 = (bf16[1,32,7168]{2,1,0:T(8,128)(2,1)}, bf16[1,32,7168]{2,1,0:T(8,128)(2,1)S(1)}, u32[]{:S(2)}, u32[]{:S(2)}) collective-permute-start(bf16[1,32,7168]{2,1,0:T(8,128)(2,1)} %get-tuple-element.23), channel_id=1, source_target_pairs={{0,4},{1,5},{2,6},{3,7},{4,0},{5,1},{6,2},{7,3},{8,12},{9,13},{10,... | collective-permute-start | bytes 1376264 | tf_op jit(solution)/shard_map/ppermute | solution.py:33
  21.2 34.5 %collective-permute-start.4 = (bf16[1,32,7168]{2,1,0:T(8,128)(2,1)}, bf16[1,32,7168]{2,1,0:T(8,128)(2,1)S(1)}, u32[]{:S(2)}, u32[]{:S(2)}) collective-permute-start(bf16[1,32,7168]{2,1,0:T(8,128)(2,1)} %get-tuple-element.22), channel_id=1, source_target_pairs={{0,5},{1,4},{2,7},{3,6},{4,1},{5,0},{6,3},{7,2},{8,13},{9,12},{10,... | collective-permute-start | bytes 1376264 | tf_op jit(solution)/shard_map/ppermute | solution.py:33
  28.7 225.9 %all-to-all-start.1 = ((bf16[16,32,7168]{2,1,0:T(8,128)(2,1)}), bf16[16,32,7168]{2,1,0:T(8,128)(2,1)}, u32[]{:S(2)}, u32[]{:S(2)}) async-start(bf16[16,32,7168]{2,1,0:T(8,128)(2,1)} %bitcast.206), calls=%async_computation.1 | async-start | bytes 14680064 | tf_op jit(solution)/shard_map/all_to_all | solution.py:119
  36.7 19.1 %copy-start.24 = (bf16[1,32,7168]{2,1,0:T(8,128)(2,1)S(1)}, bf16[1,32,7168]{2,1,0:T(8,128)(2,1)}, u32[]{:S(2)}) copy-start(bf16[1,32,7168]{2,1,0:T(8,128)(2,1)} %get-tuple-element.17) | copy-start | bytes 1376260
  36.7 127.7 %copy-start.23 = (bf16[1,32,7168]{2,1,0:T(8,128)(2,1)S(1)}, bf16[1,32,7168]{2,1,0:T(8,128)(2,1)}, u32[]{:S(2)}) copy-start(bf16[1,32,7168]{2,1,0:T(8,128)(2,1)} %get-tuple-element.16) | copy-start | bytes 1376260
  36.7 143.1 %copy-start.22 = (bf16[1,32,7168]{2,1,0:T(8,128)(2,1)S(1)}, bf16[1,32,7168]{2,1,0:T(8,128)(2,1)}, u32[]{:S(2)}) copy-start(bf16[1,32,7168]{2,1,0:T(8,128)(2,1)} %get-tuple-element.15) | copy-start | bytes 1376260
  36.7 143.9 %copy-start.21 = (bf16[1,32,7168]{2,1,0:T(8,128)(2,1)S(1)}, bf16[1,32,7168]{2,1,0:T(8,128)(2,1)}, u32[]{:S(2)}) copy-start(bf16[1,32,7168]{2,1,0:T(8,128)(2,1)} %get-tuple-element.14) | copy-start | bytes 1376260
  37.5 126.9 %collective-permute-start.5 = (bf16[1,32,7168]{2,1,0:T(8,128)(2,1)}, bf16[1,32,7168]{2,1,0:T(8,128)(2,1)S(1)}, u32[]{:S(2)}, u32[]{:S(2)}) collective-permute-start(bf16[1,32,7168]{2,1,0:T(8,128)(2,1)} %get-tuple-element.21), channel_id=1, source_target_pairs={{0,6},{1,7},{2,4},{3,5},{4,2},{5,3},{6,0},{7,1},{8,14},{9,15},{10,... | collective-permute-start | bytes 1376264 | tf_op jit(solution)/shard_map/ppermute | solution.py:33
  41.8 148.0 %copy-start.20 = (bf16[1,32,7168]{2,1,0:T(8,128)(2,1)S(1)}, bf16[1,32,7168]{2,1,0:T(8,128)(2,1)}, u32[]{:S(2)}) copy-start(bf16[1,32,7168]{2,1,0:T(8,128)(2,1)} %get-tuple-element.13) | copy-start | bytes 1376260
  43.7 155.9 %copy-start.19 = (bf16[1,32,7168]{2,1,0:T(8,128)(2,1)S(1)}, bf16[1,32,7168]{2,1,0:T(8,128)(2,1)}, u32[]{:S(2)}) copy-start(bf16[1,32,7168]{2,1,0:T(8,128)(2,1)} %get-tuple-element.12) | copy-start | bytes 1376260
  43.7 136.1 %collective-permute-start.6 = (bf16[1,32,7168]{2,1,0:T(8,128)(2,1)}, bf16[1,32,7168]{2,1,0:T(8,128)(2,1)S(1)}, u32[]{:S(2)}, u32[]{:S(2)}) collective-permute-start(bf16[1,32,7168]{2,1,0:T(8,128)(2,1)} %get-tuple-element.20), channel_id=1, source_target_pairs={{0,7},{1,6},{2,5},{3,4},{4,3},{5,2},{6,1},{7,0},{8,15},{9,14},{10,... | collective-permute-start | bytes 1376264 | tf_op jit(solution)/shard_map/ppermute | solution.py:33
  45.7 134.9 %collective-permute-start.7 = (bf16[1,32,7168]{2,1,0:T(8,128)(2,1)}, bf16[1,32,7168]{2,1,0:T(8,128)(2,1)S(1)}, u32[]{:S(2)}, u32[]{:S(2)}) collective-permute-start(bf16[1,32,7168]{2,1,0:T(8,128)(2,1)} %get-tuple-element.19), channel_id=1, source_target_pairs={{0,8},{1,9},{2,10},{3,11},{4,12},{5,13},{6,14},{7,15},{8,0},{9,1},... | collective-permute-start | bytes 1376264 | tf_op jit(solution)/shard_map/ppermute | solution.py:33
  49.5 140.4 %collective-permute-start.8 = (bf16[1,32,7168]{2,1,0:T(8,128)(2,1)}, bf16[1,32,7168]{2,1,0:T(8,128)(2,1)S(1)}, u32[]{:S(2)}, u32[]{:S(2)}) collective-permute-start(bf16[1,32,7168]{2,1,0:T(8,128)(2,1)} %get-tuple-element.18), channel_id=1, source_target_pairs={{0,9},{1,8},{2,11},{3,10},{4,13},{5,12},{6,15},{7,14},{8,1},{9,0},... | collective-permute-start | bytes 1376264 | tf_op jit(solution)/shard_map/ppermute | solution.py:33
  55.7 143.9 %collective-permute-start.9 = (bf16[1,32,7168]{2,1,0:T(8,128)(2,1)S(1)}, bf16[1,32,7168]{2,1,0:T(8,128)(2,1)S(1)}, u32[]{:S(2)}, u32[]{:S(2)}) collective-permute-start(bf16[1,32,7168]{2,1,0:T(8,128)(2,1)S(1)} %copy-done.24), channel_id=1, source_target_pairs={{0,10},{1,11},{2,8},{3,9},{4,14},{5,15},{6,12},{7,13},{8,2},{9,3},... | collective-permute-start | bytes 1376264 | tf_op jit(solution)/shard_map/ppermute | solution.py:33
  164.4 45.9 %collective-permute-start.10 = (bf16[1,32,7168]{2,1,0:T(8,128)(2,1)S(1)}, bf16[1,32,7168]{2,1,0:T(8,128)(2,1)S(1)}, u32[]{:S(2)}, u32[]{:S(2)}) collective-permute-start(bf16[1,32,7168]{2,1,0:T(8,128)(2,1)S(1)} %copy-done.23), channel_id=1, source_target_pairs={{0,11},{1,10},{2,9},{3,8},{4,15},{5,14},{6,13},{7,12},{8,3},{9,2},... | collective-permute-start | bytes 1376264 | tf_op jit(solution)/shard_map/ppermute | solution.py:33
  179.8 52.6 %collective-permute-start.11 = (bf16[1,32,7168]{2,1,0:T(8,128)(2,1)S(1)}, bf16[1,32,7168]{2,1,0:T(8,128)(2,1)S(1)}, u32[]{:S(2)}, u32[]{:S(2)}) collective-permute-start(bf16[1,32,7168]{2,1,0:T(8,128)(2,1)S(1)} %copy-done.22), channel_id=1, source_target_pairs={{0,12},{1,13},{2,14},{3,15},{4,8},{5,9},{6,10},{7,11},{8,4},{9,5},... | collective-permute-start | bytes 1376264 | tf_op jit(solution)/shard_map/ppermute | solution.py:33
  180.6 52.5 %collective-permute-start.12 = (bf16[1,32,7168]{2,1,0:T(8,128)(2,1)S(1)}, bf16[1,32,7168]{2,1,0:T(8,128)(2,1)S(1)}, u32[]{:S(2)}, u32[]{:S(2)}) collective-permute-start(bf16[1,32,7168]{2,1,0:T(8,128)(2,1)S(1)} %copy-done.21), channel_id=1, source_target_pairs={{0,13},{1,12},{2,15},{3,14},{4,9},{5,8},{6,11},{7,10},{8,5},{9,4},... | collective-permute-start | bytes 1376264 | tf_op jit(solution)/shard_map/ppermute | solution.py:33
  189.9 44.1 %collective-permute-start.13 = (bf16[1,32,7168]{2,1,0:T(8,128)(2,1)S(1)}, bf16[1,32,7168]{2,1,0:T(8,128)(2,1)S(1)}, u32[]{:S(2)}, u32[]{:S(2)}) collective-permute-start(bf16[1,32,7168]{2,1,0:T(8,128)(2,1)S(1)} %copy-done.20), channel_id=1, source_target_pairs={{0,14},{1,15},{2,12},{3,13},{4,10},{5,11},{6,8},{7,9},{8,6},{9,7},... | collective-permute-start | bytes 1376264 | tf_op jit(solution)/shard_map/ppermute | solution.py:33
  199.6 35.2 %collective-permute-start.14 = (bf16[1,32,7168]{2,1,0:T(8,128)(2,1)S(1)}, bf16[1,32,7168]{2,1,0:T(8,128)(2,1)S(1)}, u32[]{:S(2)}, u32[]{:S(2)}) collective-permute-start(bf16[1,32,7168]{2,1,0:T(8,128)(2,1)S(1)} %copy-done.19), channel_id=1, source_target_pairs={{0,15},{1,14},{2,13},{3,12},{4,11},{5,10},{6,9},{7,8},{8,7},{9,6},... | collective-permute-start | bytes 1376264 | tf_op jit(solution)/shard_map/ppermute | solution.py:33
  242.6 4.2 copy-start.12
  246.4 5.9 copy-start.4
  246.4 7.0 %copy-start.2 = (bf16[16,1,16,7168]{3,2,1,0:T(8,128)(2,1)}, bf16[16,1,16,7168]{3,2,1,0:T(8,128)(2,1)S(1)}, u32[]{:S(2)}) copy-start(bf16[16,1,16,7168]{3,2,1,0:T(8,128)(2,1)S(1)} %get-tuple-element.10) | copy-start | bytes 11010052
  246.4 4.8 copy-start.14
  254.6 4.2 copy-start.16
  258.4 5.9 copy-start.6
  258.4 5.9 copy-start.8
  258.4 4.8 copy-start.15
  265.4 2.0 copy-start.13
  273.5 121.0 %all-to-all-start.2 = ((bf16[16,32,7168]{2,1,0:T(8,128)(2,1)}), bf16[16,32,7168]{2,1,0:T(8,128)(2,1)}, u32[]{:S(2)}, u32[]{:S(2)}) async-start(bf16[16,32,7168]{2,1,0:T(8,128)(2,1)} %bitcast.208), calls=%async_computation.2 | async-start | bytes 14680064 | tf_op jit(solution)/shard_map/all_to_all | solution.py:141
  285.4 7.6 %copy-start.3 = (bf16[16,1,16,7168]{3,2,1,0:T(8,128)(2,1)S(1)}, bf16[16,1,16,7168]{3,2,1,0:T(8,128)(2,1)}, u32[]{:S(2)}) copy-start(bf16[16,1,16,7168]{3,2,1,0:T(8,128)(2,1)} %copy-done.2) | copy-start | bytes 11010052
  289.6 200.2 %collective-permute-start.17 = (bf16[128,7168]{1,0:T(8,128)(2,1)}, bf16[128,7168]{1,0:T(8,128)(2,1)}, u32[]{:S(2)}, u32[]{:S(2)}) collective-permute-start(bf16[128,7168]{1,0:T(8,128)(2,1)} %convolution_convert_fusion.4), channel_id=1, source_target_pairs={{0,8},{8,0},{1,9},{9,1},{2,10},{10,2},{3,11},{11,3},{4,12},{12,4},... | collective-permute-start | bytes 5505032 | tf_op jit(solution)/shard_map/ppermute | solution.py:47
  295.5 2.4 copy-start.5
  300.3 2.0 copy-start.7
  301.5 6.3 copy-start.17
  304.3 190.4 %collective-permute-start.16 = (bf16[7168,128]{1,0:T(8,128)(2,1)}, bf16[7168,128]{1,0:T(8,128)(2,1)}, u32[]{:S(2)}, u32[]{:S(2)}) collective-permute-start(bf16[7168,128]{1,0:T(8,128)(2,1)} %convolution_convert_fusion.6), channel_id=1, source_target_pairs={{0,8},{8,0},{1,9},{9,1},{2,10},{10,2},{3,11},{11,3},{4,12},{12,4},... | collective-permute-start | bytes 5505032 | tf_op jit(solution)/shard_map/ppermute | solution.py:47
  304.4 194.1 %collective-permute-start.15 = (bf16[7168,128]{1,0:T(8,128)(2,1)S(1)}, bf16[7168,128]{1,0:T(8,128)(2,1)}, u32[]{:S(2)}, u32[]{:S(2)}) collective-permute-start(bf16[7168,128]{1,0:T(8,128)(2,1)S(1)} %convolution_convert_fusion.8), channel_id=1, source_target_pairs={{0,8},{8,0},{1,9},{9,1},{2,10},{10,2},{3,11},{11,3},{4,12},{12,4},... | collective-permute-start | bytes 5505032 | tf_op jit(solution)/shard_map/ppermute | solution.py:47
  394.5 204.2 %all-to-all-start = ((bf16[16,32,7168]{2,1,0:T(8,128)(2,1)}), bf16[16,32,7168]{2,1,0:T(8,128)(2,1)}, u32[]{:S(2)}, u32[]{:S(2)}) async-start(bf16[16,32,7168]{2,1,0:T(8,128)(2,1)} %bitcast.207), calls=%async_computation | async-start | bytes 14680064 | tf_op jit(solution)/shard_map/all_to_all | solution.py:140
  489.6 138.3 %reduce-scatter.9.cloned.1.call-start = ((), (), s32[]{:S(2)}) async-start(), calls=%async_computation.6 | async-start | bytes 2064384
  489.9 2.6 copy-start.11
  506.2 1.9 copy-start.10
  507.9 134.6 %reduce-scatter.7.cloned.1.call-start = ((), (), s32[]{:S(2)}) async-start(), calls=%async_computation.5 | async-start | bytes 2064384
  608.6 35.6 %copy-start.1 = (bf16[32,7168]{1,0:T(8,128)(2,1)S(1)}, bf16[32,7168]{1,0:T(8,128)(2,1)}, u32[]{:S(2)}) copy-start(bf16[32,7168]{1,0:T(8,128)(2,1)} %param.8) | copy-start | bytes 1376260
  (2 other events, 2.7 us)
Sparse Core Ops, SparseCore 0:
  508.0 39.7 reduce-scatter.8
  608.5 33.9 reduce-scatter.6
